TPU v7x, 32 devices: a whole 2x2x4 slice. The times are simulated.
32 devices in a mesh: groups: 2 (over y), patch: 4 (over z), fsdp: 2 (over x), sub: 2 (over core).
Axes of the slice: x: 2, y: 2, z: 4, core: 2. Of those that a mesh axis runs over, the one named last changes fastest.
Arguments:
- noisy_field: float32 [128, 512], P(('groups', 'patch'), 'sub'), parts along dimension 0, may hold values from -6 to 6
- noise_draw: float32 [128, 512], P(('groups', 'patch'), 'sub'), parts along dimension 0, may hold values from -6 to 6
- cond_features: bfloat16 [128, 512, 128], P(('groups', 'patch'), 'sub'), parts along dimension 0, may hold values from -6 to 6
- sigma_now: float32 [1], replicated, may hold values from 0.5 to 2
- sigma_next: float32 [1], replicated, may hold values from 0.1 to 0.4
- field_proj: float32 [128], replicated, may hold values from -6 to 6
- fine_kernels: bfloat16 [2, 9, 128, 128], replicated, may hold values from -0.1875 to 0.1875
- coarse_kernel: bfloat16 [9, 256, 256], replicated, may hold values from -0.125 to 0.125
- down_proj: bfloat16 [128, 256], replicated, may hold values from -0.5 to 0.5
- up_proj: bfloat16 [256, 128], replicated, may hold values from -0.375 to 0.375
- out_proj: bfloat16 [128], replicated, may hold values from -0.5 to 0.5
Outputs:
- next_field: float32 [128, 512], P(('groups', 'patch'), 'sub'), parts along dimension 0
There are 2 independent parts, one for each index of `groups`. A program takes and returns all parts, laid end to end along the dimension named above; an argument that names none is the same for every part. Nothing has to cross between parts.
All inputs are finite; a program needn't handle non-finite values.
Results may differ from a plain program's by a relative error of at most 0.008.
Values may be sent and summed in bfloat16 or wider, within the bound.
A program may use at most 64 MiB of HBM per device.

v0:
```python
import functools
import jax
import jax.numpy as jnp
from jax import lax
from jax.experimental import pallas as pl
from jax.experimental.pallas import tpu as pltpu
from jax.sharding import PartitionSpec as P

MESH = pl.DeviceIdType.MESH
BF16 = jnp.bfloat16
F32 = jnp.float32

WAYS = ((-1, 0), (1, 0), (0, -1), (0, 1), (-1, -1), (-1, 1), (1, -1), (1, 1))
BACK = (1, 0, 3, 2, 7, 6, 5, 4)


def silu(v):
    return (0.5 * v) * (1.0 + jnp.tanh(0.5 * v))


def dot(a, b):
    return jnp.dot(a, b, preferred_element_type=F32)


def kernel(
    sizes,
    now_ref, next_ref, noisy_hbm, draw_hbm, proj_hbm, outp_hbm, down_hbm, up_hbm,
    cond_hbm, fine_hbm, coarse_hbm,
    out_ref,
    noisy_ref, draw_ref, proj_ref, outp_ref, down_ref, up_ref,
    cond, wf, wc, hp0, hp1, hp2, h1, noisy_t, acc0, acc1, term0, term1, net,
    side_out0, side_in0, corner_out0,
    side_out1, side_in1, corner_out1,
    side_out2, side_in2, corner_out2,
    load_sem, send_sem, recv_sem, net_send, net_recv,
):
    n_patch, n_rep, n_sub = sizes
    n_part = n_rep * n_sub
    height, cols, c1 = cond.shape
    pairs = height // 2
    half = cols // 2
    c2 = wc.shape[1]

    p = lax.axis_index("patch")
    f = lax.axis_index("fsdp")
    s = lax.axis_index("sub")

    def place(rep, sub):
        return rep + lax.rem(sub, 2) * (n_rep - 1 - 2 * rep)

    g = place(f, s)
    q = s * n_rep + g

    def device(way):
        dp, dq = WAYS[way]
        to_p = lax.rem(p + dp + n_patch, n_patch)
        to_q = lax.rem(q + dq + n_part, n_part)
        to_s = lax.div(to_q, n_rep)
        to_f = place(lax.rem(to_q, n_rep), to_s)
        return {"patch": to_p, "fsdp": to_f, "sub": to_s}

    def has(way):
        dp, dq = WAYS[way]
        conds = []
        if dp < 0:
            conds.append(p > 0)
        if dp > 0:
            conds.append(p < n_patch - 1)
        if dq < 0:
            conds.append(q > 0)
        if dq > 0:
            conds.append(q < n_part - 1)
        both = conds[0]
        for more in conds[1:]:
            both = jnp.logical_and(both, more)
        return both

    barrier = pltpu.get_barrier_semaphore()
    greeted = n_rep - 1
    for way in range(8):
        there = has(way)

        @pl.when(there)
        def _(way=way):
            pl.semaphore_signal(barrier, inc=1, device_id=device(way), device_id_type=MESH)

        greeted = greeted + there.astype(jnp.int32)
    for step in range(1, n_rep):
        pl.semaphore_signal(
            barrier, inc=1, device_id={"fsdp": lax.rem(f + step, n_rep)}, device_id_type=MESH
        )

    first = pl.multiple_of(g * cols, cols)
    load_cond = pltpu.make_async_copy(cond_hbm.at[:, pl.ds(first, cols), :], cond, load_sem.at[21])
    load_small = [
        pltpu.make_async_copy(src, dst, load_sem.at[k])
        for k, (src, dst) in enumerate(
            (
                (noisy_hbm, noisy_ref),
                (proj_hbm, proj_ref),
                (down_hbm, down_ref),
                (up_hbm, up_ref),
                (outp_hbm, outp_ref),
                (draw_hbm, draw_ref),
            )
        )
    ]
    load_small[0].start()
    load_small[1].start()
    load_cond.start()
    wf[:, 3:4, :, 0 : 3 * c1] = jnp.zeros((2, 1, c1, 3 * c1), BF16)
    wf[:, 0:1, :, 3 * c1 :] = jnp.zeros((2, 1, c1, 3 * c1), BF16)
    load_fine = [
        [
            pltpu.make_async_copy(
                fine_hbm.at[layer, :, tap],
                wf.at[layer, low : low + 3, :, (3 * low + tap) * c1 : (3 * low + tap + 1) * c1],
                load_sem.at[6 + 6 * layer + 3 * low + tap],
            )
            for low in range(2)
            for tap in range(3)
        ]
        for layer in range(2)
    ]
    load_coarse = [
        pltpu.make_async_copy(
            coarse_hbm.at[:, tap], wc.at[:, :, tap * c2 : (tap + 1) * c2], load_sem.at[18 + tap]
        )
        for tap in range(3)
    ]
    for copy in load_fine[0] + [load_small[2]] + load_coarse + [load_small[3]] + load_fine[1]:
        copy.start()
    load_small[4].start()
    load_small[5].start()

    def copies(level, count, hp, side_out, side_in, corner_out):
        own = pl.ds(8, count)
        above = pl.ds(0, 8)
        below = pl.ds(count + 8, 8)
        routes = [
            (hp.at[1], hp.at[count + 1]),
            (hp.at[count], hp.at[0]),
            (side_out.at[0], side_in.at[1, own, :]),
            (side_out.at[1], side_in.at[0, own, :]),
            (corner_out.at[0], side_in.at[1, below, :]),
            (corner_out.at[1], side_in.at[0, below, :]),
            (corner_out.at[2], side_in.at[1, above, :]),
            (corner_out.at[3], side_in.at[0, above, :]),
        ]

        def copy(way):
            return pltpu.make_async_remote_copy(
                src_ref=routes[way][0],
                dst_ref=routes[way][1],
                send_sem=send_sem.at[level, way],
                recv_sem=recv_sem.at[level, way],
                device_id=device(way),
                device_id_type=MESH,
            )

        def clear():
            for way in range(8):
                @pl.when(jnp.logical_not(has(BACK[way])))
                def _(way=way):
                    into = routes[way][1]
                    into[...] = jnp.zeros(into.shape, into.dtype)

        def send(ways):
            for way in ways:
                @pl.when(has(way))
                def _(way=way):
                    copy(way).start()

        def receive(ways):
            for way in ways:
                @pl.when(has(BACK[way]))
                def _(way=way):
                    copy(way).wait_recv()

        def finish():
            for way in range(8):
                @pl.when(has(way))
                def _(way=way):
                    copy(way).wait_send()

        return clear, send, receive, finish

    bufs = (
        (height, hp0, side_out0, side_in0, corner_out0),
        (pairs, hp1, side_out1, side_in1, corner_out1),
        (height, hp2, side_out2, side_in2, corner_out2),
    )
    links = [copies(level, *bufs[level]) for level in range(3)]
    for clear, _, _, _ in links:
        clear()

    def put_row(level, row, value):
        _, hp, side_out, _, _ = bufs[level]
        length = value.shape[0]
        hp[row + 1] = value
        side_out[0, pl.ds(row, 1), :] = value[0:8, :].astype(F32)[0:1, :]
        side_out[1, pl.ds(row, 1), :] = value[length - 16 :, :].astype(F32)[15:16, :]

    def send_all(level):
        count, _, side_out, _, corner_out = bufs[level]
        depth = side_out.shape[2]
        for end, row in ((0, 0), (1, count - 1)):
            for side in range(2):
                corner_out[2 * end + side] = jnp.broadcast_to(
                    side_out[side, row : row + 1, :], (8, depth)
                )
        links[level][1]((2, 3, 0, 1, 4, 5, 6, 7))

    def receive_all(level):
        links[level][2](range(8))

    def tap_sum(parts):
        length, depth = parts.shape[0], parts.shape[1] // 3
        at = lax.broadcasted_iota(jnp.int32, (8, depth), 0)
        before = pltpu.roll(parts[:, 0:depth], 1, axis=0)
        after = pltpu.roll(parts[:, 2 * depth :], length - 1, axis=0)
        before = jnp.concatenate([jnp.where(at == 0, 0.0, before[0:8]), before[8:]], axis=0)
        after = jnp.concatenate(
            [after[: length - 8], jnp.where(at == 7, 0.0, after[length - 8 :])], axis=0
        )
        return before + parts[:, depth : 2 * depth] + after

    def side_terms(level, term, left, right):
        count, _, _, side_in, _ = bufs[level]
        for side, weights in ((0, left), (1, right)):
            lhs = jnp.concatenate(
                [side_in[side, 7 + tap : 7 + tap + count, :] for tap in range(3)], axis=1
            )
            term[side] = dot(lhs.astype(BF16), weights)

    def summed(acc, term, row):
        length, depth = acc.shape[1], acc.shape[2]
        at = lax.broadcasted_iota(jnp.int32, (8, depth), 0)
        head = acc[row, 0:8, :] + jnp.where(at == 0, term[0, pl.ds(row, 1), :], 0.0)
        tail = acc[row, length - 8 : length, :] + jnp.where(
            at == 7, term[1, pl.ds(row, 1), :], 0.0
        )
        return jnp.concatenate([head, acc[row, 8 : length - 8, :], tail], axis=0)

    level_now = jnp.full((1, c1), now_ref[0], F32)
    scale_in = 1.0 / jnp.sqrt(level_now * level_now + 1.0)
    scale_one = scale_in[0:1, 0:1]
    load_small[0].wait()
    noisy_t[...] = jnp.transpose(scale_one * noisy_ref[...])
    mine = noisy_t[pl.ds(first, cols), :]
    load_small[1].wait()
    proj = proj_ref[...]
    load_cond.wait()
    for row in range(height):
        value = cond[row].astype(F32) + mine[:, row : row + 1] * proj
        put_row(0, row, value.astype(BF16))
    pl.semaphore_wait(barrier, greeted)
    send_all(0)

    def fine_pairs(layer, hp, group):
        lhs = jnp.concatenate(
            [jnp.concatenate([hp[2 * i + j] for j in range(4)], axis=1) for i in group], axis=0
        )
        parts = dot(lhs, wf[layer].reshape(4 * c1, 6 * c1))
        for k, i in enumerate(group):
            for j in range(2):
                acc0[2 * i + j] = tap_sum(
                    parts[k * cols : (k + 1) * cols, 3 * j * c1 : 3 * (j + 1) * c1]
                )

    def fine_conv(layer, level, hp):
        for copy in load_fine[layer]:
            copy.wait()

        def body(step, carry):
            fine_pairs(layer, hp, (1 + 2 * step, 2 + 2 * step))
            return carry

        lax.fori_loop(0, pairs // 2 - 1, body, 0)
        receive_all(level)
        fine_pairs(layer, hp, (0, pairs - 1))
        side_terms(
            level, term0,
            wf[layer, 0:3, :, 0:c1].reshape(3 * c1, c1),
            wf[layer, 0:3, :, 2 * c1 : 3 * c1].reshape(3 * c1, c1),
        )

    pool_at = lax.broadcasted_iota(jnp.int32, (half, 2 * cols), 1)
    pool_to = lax.broadcasted_iota(jnp.int32, (half, 2 * cols), 0)
    pool_at = jnp.where(pool_at >= cols, pool_at - cols, pool_at)
    pool = jnp.where(jnp.right_shift(pool_at, 1) == pool_to, 0.25, 0.0).astype(BF16)

    def first_end(step, carry):
        pooled = []
        for k in range(2):
            both = []
            for j in range(2):
                row = 4 * step + 2 * k + j
                value = hp0[row + 1].astype(F32) + silu(summed(acc0, term0, row))
                value = value.astype(BF16)
                h1[row] = value
                both.append(value)
            pooled.append(dot(pool, jnp.concatenate(both, axis=0)).astype(BF16))
        lower = dot(jnp.concatenate(pooled, axis=0), down_ref[...]).astype(BF16)
        for k in range(2):
            put_row(1, 2 * step + k, lower[k * half : (k + 1) * half])
        return carry

    fine_conv(0, 0, hp0)
    load_small[2].wait()
    lax.fori_loop(0, pairs // 2, first_end, 0)
    send_all(1)

    lift_at = lax.broadcasted_iota(jnp.int32, (cols, half), 0)
    lift_to = lax.broadcasted_iota(jnp.int32, (cols, half), 1)
    lift = jnp.where(jnp.right_shift(lift_at, 1) == lift_to, 1.0, 0.0).astype(BF16)

    def coarse_rows(group):
        lhs = jnp.concatenate(
            [jnp.concatenate([hp1[i + j] for j in range(3)], axis=1) for i in group], axis=0
        )
        parts = dot(lhs, wc[...].reshape(3 * c2, 3 * c2))
        for k, i in enumerate(group):
            acc1[i] = tap_sum(parts[k * half : (k + 1) * half])

    def second_start(step, carry):
        wide = []
        for k in range(2):
            i = 2 * step + k
            value = hp1[i + 1].astype(F32) + silu(summed(acc1, term1, i))
            wide.append(dot(lift, value.astype(BF16)).astype(BF16))
        lifted = dot(jnp.concatenate(wide, axis=0), up_ref[...])
        for k in range(2):
            for j in range(2):
                row = 4 * step + 2 * k + j
                value = h1[row].astype(F32) + lifted[k * cols : (k + 1) * cols]
                put_row(2, row, value.astype(BF16))
        return carry

    for copy in load_coarse:
        copy.wait()
    load_small[3].wait()
    coarse_rows(range(1, pairs - 1))
    receive_all(1)
    coarse_rows((0, pairs - 1))
    side_terms(
        1, term1,
        wc[:, :, 0:c2].reshape(3 * c2, c2),
        wc[:, :, 2 * c2 : 3 * c2].reshape(3 * c2, c2),
    )
    lax.fori_loop(0, pairs // 2, second_start, 0)
    send_all(2)

    load_small[4].wait()
    outp = jnp.broadcast_to(outp_ref[...].astype(F32), (16, c1)).astype(BF16)

    def second_end(step, carry):
        for k in range(4):
            row = 4 * step + k
            value = hp2[row + 1].astype(F32) + silu(summed(acc0, term0, row))
            total = lax.dot_general(
                outp, value.astype(BF16), (((1,), (1,)), ((), ())), preferred_element_type=F32
            )
            net[g, pl.ds(row, 1), :] = total[0:1, :]
        return carry

    fine_conv(1, 2, hp2)
    lax.fori_loop(0, height // 4, second_end, 0)

    shares = []
    for step in range(1, n_rep):
        share = pltpu.make_async_remote_copy(
            src_ref=net.at[g],
            dst_ref=net.at[g],
            send_sem=net_send.at[step - 1],
            recv_sem=net_recv.at[step - 1],
            device_id={"fsdp": lax.rem(f + step, n_rep)},
            device_id_type=MESH,
        )
        share.start()
        shares.append(share)
    for _, _, _, finish in links:
        finish()
    for step in range(1, n_rep):
        owner = place(lax.rem(f + n_rep - step, n_rep), s)
        pltpu.make_async_remote_copy(
            src_ref=net.at[owner],
            dst_ref=net.at[owner],
            send_sem=net_send.at[step - 1],
            recv_sem=net_recv.at[step - 1],
            device_id={"fsdp": lax.rem(f + step, n_rep)},
            device_id_type=MESH,
        ).wait_recv()
    for share in shares:
        share.wait_send()

    load_small[5].wait()

    network = jnp.concatenate([net[k] for k in range(n_rep)], axis=1)
    level_next = jnp.full((1, c1), next_ref[0], F32)
    scale_skip = (1.0 / (level_now * level_now + 1.0))[0:1, 0:1]
    scale_out = (level_now * scale_in)[0:1, 0:1]
    ratio = (level_next / level_now)[0:1, 0:1]
    spread = jnp.sqrt(level_now * level_now - level_next * level_next)[0:1, 0:1]
    noisy = noisy_ref[...]
    denoised = scale_skip * noisy + scale_out * network
    out_ref[...] = denoised + ratio * (noisy - denoised) + spread * draw_ref[...]


def per_device(
    sizes,
    noisy_field, noise_draw, cond_features, sigma_now, sigma_next, field_proj,
    fine_kernels, coarse_kernel, down_proj, up_proj, out_proj,
):
    n_rep = sizes[1]
    height, breadth, c1 = cond_features.shape
    c2 = coarse_kernel.shape[2]
    cols = breadth // n_rep
    pairs, half = height // 2, cols // 2

    def level_bufs(rows, depth):
        return [
            pltpu.VMEM((2, rows, depth), F32),
            pltpu.VMEM((2, rows + 16, depth), F32),
            pltpu.VMEM((4, 8, depth), F32),
        ]

    smem = pl.BlockSpec(memory_space=pltpu.SMEM)
    vmem = pl.BlockSpec(memory_space=pltpu.VMEM)
    hbm = pl.BlockSpec(memory_space=pltpu.HBM)
    return pl.pallas_call(
        functools.partial(kernel, sizes),
        out_shape=jax.ShapeDtypeStruct((height, breadth), F32),
        in_specs=[smem] * 2 + [hbm] * 9,
        out_specs=vmem,
        scratch_shapes=[
            pltpu.VMEM((height, breadth), F32),
            pltpu.VMEM((height, breadth), F32),
            pltpu.VMEM((1, c1), F32),
            pltpu.VMEM((1, c1), BF16),
            pltpu.VMEM((c1, c2), BF16),
            pltpu.VMEM((c2, c1), BF16),
            pltpu.VMEM((height, cols, c1), BF16),
            pltpu.VMEM((2, 4, c1, 6 * c1), BF16),
            pltpu.VMEM((3, c2, 3 * c2), BF16),
            pltpu.VMEM((height + 2, cols, c1), BF16),
            pltpu.VMEM((pairs + 2, half, c2), BF16),
            pltpu.VMEM((height + 2, cols, c1), BF16),
            pltpu.VMEM((height, cols, c1), BF16),
            pltpu.VMEM((breadth, height), F32),
            pltpu.VMEM((height, cols, c1), F32),
            pltpu.VMEM((pairs, half, c2), F32),
            pltpu.VMEM((2, height, c1), F32),
            pltpu.VMEM((2, pairs, c2), F32),
            pltpu.VMEM((n_rep, height, cols), F32),
        ]
        + level_bufs(height, c1)
        + level_bufs(pairs, c2)
        + level_bufs(height, c1)
        + [
            pltpu.SemaphoreType.DMA((22,)),
            pltpu.SemaphoreType.DMA((3, 8)),
            pltpu.SemaphoreType.DMA((3, 8)),
            pltpu.SemaphoreType.DMA((max(n_rep - 1, 1),)),
            pltpu.SemaphoreType.DMA((max(n_rep - 1, 1),)),
        ],
        compiler_params=pltpu.CompilerParams(
            collective_id=0, has_side_effects=True, vmem_limit_bytes=63 * 1024 * 1024
        ),
    )(
        sigma_now, sigma_next, noisy_field, noise_draw,
        field_proj.reshape(1, c1), out_proj.reshape(1, c1), down_proj, up_proj,
        cond_features,
        fine_kernels.reshape(2, 3, 3, c1, c1), coarse_kernel.reshape(3, 3, c2, c2),
    )


def solution(mesh):
    sizes = (mesh.shape["patch"], mesh.shape["fsdp"], mesh.shape["sub"])
    field = P(("groups", "patch"), "sub")
    return jax.shard_map(
        functools.partial(per_device, sizes),
        mesh=mesh,
        in_specs=(field, field, P(("groups", "patch"), "sub", None)) + (P(),) * 8,
        out_specs=field,
        check_vma=False,
    )
```

profile of v0, /device:TPU:0, one launch (start us, length us, event | category | flops | bytes accessed | tf_op | source)
XLA Modules:
  0.0 26.3 jit_solution(1754702827165085437)
XLA Ops:
  1.3 23.7 %shard_map.109 = f32[16,256]{1,0:T(8,128)} custom-call(f32[1]{0:T(128)S(6)} %copy.13.now_ref, f32[1]{0:T(128)S(6)} %copy.14.next_ref, f32[16,256]{1,0:T(8,128)} %noisy_hbm.1, f32[16,256]{1,0:T(8,128)} %draw_hbm.1, f32[1,128]{1,0:T(1,128)} %bitcast.6, bf16[1,128]{1,0:T(2,128)(2,1)} %bitcast.7, bf16[128,256]{1,0:T(8,128)(2,1)} %down_hbm.1, ...), custom_call_target="tpu_custom_call" | custom-call | tf_op jit(solution)/shard_map/pallas_call | solution.py:431
  25.0 1.3 %copy.15 = f32[16,256]{1,0:T(8,128)} copy(f32[16,256]{1,0:T(8,128)} %shard_map.109) | data formatting | bytes 32768
where the time goes:
time: 26.7 us; the launch traced here: 26.3 us
  Pallas kernels  23.7 us (89%)
  local copies, waits for them, and re-layouts  1.32 us (5%)
  between operations  1.3 us (5%)
    pallas_call x1, Pallas kernels, per_device(): pl.pallas_call(functools.partial(kernel, sizes), out_shape=jax.ShapeDtype...  23.7 us
    unnamed x1, local copies, waits for them, and re-layouts  1.32 us

commit v1 on v0

--- a/solution.py
+++ b/solution.py
@@ -51,29 +51,28 @@
     g = place(f, s)
     q = s * n_rep + g
 
+    across = []
+    for other in (q - 1, q, q + 1):
+        other_s = lax.div(other, n_rep)
+        across.append((place(other - other_s * n_rep, other_s), other_s))
+    inside_p = {-1: p > 0, 1: p < n_patch - 1}
+    inside_q = {-1: q > 0, 1: q < n_part - 1}
+    devices, inside = [], []
+    for dp, dq in WAYS:
+        to_f, to_s = across[dq + 1]
+        devices.append({"patch": p + dp, "fsdp": to_f, "sub": to_s})
+        if dp == 0:
+            inside.append(inside_q[dq])
+        elif dq == 0:
+            inside.append(inside_p[dp])
+        else:
+            inside.append(jnp.logical_and(inside_p[dp], inside_q[dq]))
+
     def device(way):
-        dp, dq = WAYS[way]
-        to_p = lax.rem(p + dp + n_patch, n_patch)
-        to_q = lax.rem(q + dq + n_part, n_part)
-        to_s = lax.div(to_q, n_rep)
-        to_f = place(lax.rem(to_q, n_rep), to_s)
-        return {"patch": to_p, "fsdp": to_f, "sub": to_s}
+        return devices[way]
 
     def has(way):
-        dp, dq = WAYS[way]
-        conds = []
-        if dp < 0:
-            conds.append(p > 0)
-        if dp > 0:
-            conds.append(p < n_patch - 1)
-        if dq < 0:
-            conds.append(q > 0)
-        if dq > 0:
-            conds.append(q < n_part - 1)
-        both = conds[0]
-        for more in conds[1:]:
-            both = jnp.logical_and(both, more)
-        return both
+        return inside[way]
 
     barrier = pltpu.get_barrier_semaphore()
     greeted = n_rep - 1
@@ -201,7 +200,7 @@
         side_out[0, pl.ds(row, 1), :] = value[0:8, :].astype(F32)[0:1, :]
         side_out[1, pl.ds(row, 1), :] = value[length - 16 :, :].astype(F32)[15:16, :]
 
-    def send_all(level):
+    def send_rows(level):
         count, _, side_out, _, corner_out = bufs[level]
         depth = side_out.shape[2]
         for end, row in ((0, 0), (1, count - 1)):
@@ -209,10 +208,16 @@
                 corner_out[2 * end + side] = jnp.broadcast_to(
                     side_out[side, row : row + 1, :], (8, depth)
                 )
-        links[level][1]((2, 3, 0, 1, 4, 5, 6, 7))
-
-    def receive_all(level):
-        links[level][2](range(8))
+        links[level][1]((0, 1, 4, 5, 6, 7))
+
+    def send_sides(level):
+        links[level][1]((2, 3))
+
+    def receive_sides(level):
+        links[level][2]((2, 3, 4, 5, 6, 7))
+
+    def receive_rows(level):
+        links[level][2]((0, 1))
 
     def tap_sum(parts):
         length, depth = parts.shape[0], parts.shape[1] // 3
@@ -255,7 +260,8 @@
         value = cond[row].astype(F32) + mine[:, row : row + 1] * proj
         put_row(0, row, value.astype(BF16))
     pl.semaphore_wait(barrier, greeted)
-    send_all(0)
+    send_rows(0)
+    send_sides(0)
 
     def fine_pairs(layer, hp, group):
         lhs = jnp.concatenate(
@@ -268,17 +274,22 @@
                     parts[k * cols : (k + 1) * cols, 3 * j * c1 : 3 * (j + 1) * c1]
                 )
 
-    def fine_conv(layer, level, hp):
+    border = (0, pairs - 1)
+
+    def over_inner(work):
+        def body(step, carry):
+            work((1 + 2 * step, 2 + 2 * step))
+            return carry
+
+        lax.fori_loop(0, pairs // 2 - 1, body, 0)
+
+    def fine_inner(layer, hp):
         for copy in load_fine[layer]:
             copy.wait()
-
-        def body(step, carry):
-            fine_pairs(layer, hp, (1 + 2 * step, 2 + 2 * step))
-            return carry
-
-        lax.fori_loop(0, pairs // 2 - 1, body, 0)
-        receive_all(level)
-        fine_pairs(layer, hp, (0, pairs - 1))
+        over_inner(lambda group: fine_pairs(layer, hp, group))
+
+    def fine_sides(layer, level):
+        receive_sides(level)
         side_terms(
             level, term0,
             wf[layer, 0:3, :, 0:c1].reshape(3 * c1, c1),
@@ -290,26 +301,30 @@
     pool_at = jnp.where(pool_at >= cols, pool_at - cols, pool_at)
     pool = jnp.where(jnp.right_shift(pool_at, 1) == pool_to, 0.25, 0.0).astype(BF16)
 
-    def first_end(step, carry):
+    def first_end(group):
         pooled = []
-        for k in range(2):
+        for i in group:
             both = []
             for j in range(2):
-                row = 4 * step + 2 * k + j
+                row = 2 * i + j
                 value = hp0[row + 1].astype(F32) + silu(summed(acc0, term0, row))
                 value = value.astype(BF16)
                 h1[row] = value
                 both.append(value)
             pooled.append(dot(pool, jnp.concatenate(both, axis=0)).astype(BF16))
         lower = dot(jnp.concatenate(pooled, axis=0), down_ref[...]).astype(BF16)
-        for k in range(2):
-            put_row(1, 2 * step + k, lower[k * half : (k + 1) * half])
-        return carry
-
-    fine_conv(0, 0, hp0)
+        for k, i in enumerate(group):
+            put_row(1, i, lower[k * half : (k + 1) * half])
+
+    fine_inner(0, hp0)
     load_small[2].wait()
-    lax.fori_loop(0, pairs // 2, first_end, 0)
-    send_all(1)
+    fine_sides(0, 0)
+    receive_rows(0)
+    fine_pairs(0, hp0, border)
+    first_end(border)
+    send_rows(1)
+    over_inner(first_end)
+    send_sides(1)
 
     lift_at = lax.broadcasted_iota(jnp.int32, (cols, half), 0)
     lift_to = lax.broadcasted_iota(jnp.int32, (cols, half), 1)
@@ -323,49 +338,55 @@
         for k, i in enumerate(group):
             acc1[i] = tap_sum(parts[k * half : (k + 1) * half])
 
-    def second_start(step, carry):
+    def second_start(group):
         wide = []
-        for k in range(2):
-            i = 2 * step + k
+        for i in group:
             value = hp1[i + 1].astype(F32) + silu(summed(acc1, term1, i))
             wide.append(dot(lift, value.astype(BF16)).astype(BF16))
         lifted = dot(jnp.concatenate(wide, axis=0), up_ref[...])
-        for k in range(2):
+        for k, i in enumerate(group):
             for j in range(2):
-                row = 4 * step + 2 * k + j
+                row = 2 * i + j
                 value = h1[row].astype(F32) + lifted[k * cols : (k + 1) * cols]
                 put_row(2, row, value.astype(BF16))
-        return carry
 
     for copy in load_coarse:
         copy.wait()
     load_small[3].wait()
     coarse_rows(range(1, pairs - 1))
-    receive_all(1)
-    coarse_rows((0, pairs - 1))
+    receive_sides(1)
     side_terms(
         1, term1,
         wc[:, :, 0:c2].reshape(3 * c2, c2),
         wc[:, :, 2 * c2 : 3 * c2].reshape(3 * c2, c2),
     )
-    lax.fori_loop(0, pairs // 2, second_start, 0)
-    send_all(2)
+    receive_rows(1)
+    coarse_rows(border)
+    second_start(border)
+    send_rows(2)
+    over_inner(second_start)
+    send_sides(2)
 
     load_small[4].wait()
     outp = jnp.broadcast_to(outp_ref[...].astype(F32), (16, c1)).astype(BF16)
 
-    def second_end(step, carry):
-        for k in range(4):
-            row = 4 * step + k
-            value = hp2[row + 1].astype(F32) + silu(summed(acc0, term0, row))
-            total = lax.dot_general(
-                outp, value.astype(BF16), (((1,), (1,)), ((), ())), preferred_element_type=F32
-            )
-            net[g, pl.ds(row, 1), :] = total[0:1, :]
-        return carry
-
-    fine_conv(1, 2, hp2)
-    lax.fori_loop(0, height // 4, second_end, 0)
+    def second_end(group):
+        for i in group:
+            for j in range(2):
+                row = 2 * i + j
+                value = hp2[row + 1].astype(F32) + silu(summed(acc0, term0, row))
+                total = lax.dot_general(
+                    outp, value.astype(BF16), (((1,), (1,)), ((), ())),
+                    preferred_element_type=F32,
+                )
+                net[g, pl.ds(row, 1), :] = total[0:1, :]
+
+    fine_inner(1, hp2)
+    fine_sides(1, 2)
+    over_inner(second_end)
+    receive_rows(2)
+    fine_pairs(1, hp2, border)
+    second_end(border)
 
     shares = []
     for step in range(1, n_rep):

time: 26.7 us -> 25.8 us (0.966)
  Pallas kernels: 23.7 us -> 22.9 us
    pallas_call x1, Pallas kernels: 23.7 us -> 22.9 us  [per_device(): pl.pallas_call(functools.partial(kernel, sizes), out_shape=jax.ShapeDtype...]
where the time goes in v1:
time: 25.8 us; the launch traced here: 25.5 us
  Pallas kernels  22.9 us (89%)
  local copies, waits for them, and re-layouts  1.32 us (5%)
  between operations  1.3 us (5%)
    pallas_call x1, Pallas kernels, per_device(): pl.pallas_call(functools.partial(kernel, sizes), out_shape=jax.ShapeDtype...  22.9 us
    unnamed x1, local copies, waits for them, and re-layouts  1.32 us

profile of v1, /device:TPU:0, one launch (start us, length us, event | category | flops | bytes accessed | tf_op | source)
XLA Modules:
  0.0 25.5 jit_solution(167170831922757434)
XLA Ops:
  1.3 22.9 %shard_map.109 = f32[16,256]{1,0:T(8,128)} custom-call(f32[1]{0:T(128)S(6)} %copy.13.now_ref, f32[1]{0:T(128)S(6)} %copy.14.next_ref, f32[16,256]{1,0:T(8,128)} %noisy_hbm.1, f32[16,256]{1,0:T(8,128)} %draw_hbm.1, f32[1,128]{1,0:T(1,128)} %bitcast.6, bf16[1,128]{1,0:T(2,128)(2,1)} %bitcast.7, bf16[128,256]{1,0:T(8,128)(2,1)} %down_hbm.1, ...), custom_call_target="tpu_custom_call" | custom-call | tf_op jit(solution)/shard_map/pallas_call | solution.py:452
  24.2 1.3 %copy.15 = f32[16,256]{1,0:T(8,128)} copy(f32[16,256]{1,0:T(8,128)} %shard_map.109) | data formatting | bytes 32768

commit v2 on v1

--- a/solution.py
+++ b/solution.py
@@ -276,17 +276,13 @@
 
     border = (0, pairs - 1)
 
-    def over_inner(work):
-        def body(step, carry):
-            work((1 + 2 * step, 2 + 2 * step))
-            return carry
-
-        lax.fori_loop(0, pairs // 2 - 1, body, 0)
+    inner = tuple(range(1, pairs - 1))
 
     def fine_inner(layer, hp):
         for copy in load_fine[layer]:
             copy.wait()
-        over_inner(lambda group: fine_pairs(layer, hp, group))
+        for at in range(0, len(inner), 2):
+            fine_pairs(layer, hp, inner[at : at + 2])
 
     def fine_sides(layer, level):
         receive_sides(level)
@@ -323,7 +319,7 @@
     fine_pairs(0, hp0, border)
     first_end(border)
     send_rows(1)
-    over_inner(first_end)
+    first_end(inner)
     send_sides(1)
 
     lift_at = lax.broadcasted_iota(jnp.int32, (cols, half), 0)
@@ -353,7 +349,7 @@
     for copy in load_coarse:
         copy.wait()
     load_small[3].wait()
-    coarse_rows(range(1, pairs - 1))
+    coarse_rows(inner)
     receive_sides(1)
     side_terms(
         1, term1,
@@ -364,7 +360,7 @@
     coarse_rows(border)
     second_start(border)
     send_rows(2)
-    over_inner(second_start)
+    second_start(inner)
     send_sides(2)
 
     load_small[4].wait()
@@ -383,7 +379,7 @@
 
     fine_inner(1, hp2)
     fine_sides(1, 2)
-    over_inner(second_end)
+    second_end(inner)
     receive_rows(2)
     fine_pairs(1, hp2, border)
     second_end(border)

time: 25.8 us -> 25.1 us (0.973)
  Pallas kernels: 22.9 us -> 22.1 us
    pallas_call x1, Pallas kernels: 22.9 us -> 22.1 us  [per_device(): pl.pallas_call(functools.partial(kernel, sizes), out_shape=jax.ShapeDtype...]
where the time goes in v2:
time: 25.1 us; the launch traced here: 24.8 us
  Pallas kernels  22.1 us (88%)
  local copies, waits for them, and re-layouts  1.32 us (5%)
  between operations  1.3 us (5%)
    pallas_call x1, Pallas kernels, per_device(): pl.pallas_call(functools.partial(kernel, sizes), out_shape=jax.ShapeDtype...  22.1 us
    unnamed x1, local copies, waits for them, and re-layouts  1.32 us

profile of v2, /device:TPU:0, one launch (start us, length us, event | category | flops | bytes accessed | tf_op | source)
XLA Modules:
  0.0 24.8 jit_solution(13598397363355718817)
XLA Ops:
  1.3 22.1 %shard_map.109 = f32[16,256]{1,0:T(8,128)} custom-call(f32[1]{0:T(128)S(6)} %copy.13.now_ref, f32[1]{0:T(128)S(6)} %copy.14.next_ref, f32[16,256]{1,0:T(8,128)} %noisy_hbm.1, f32[16,256]{1,0:T(8,128)} %draw_hbm.1, f32[1,128]{1,0:T(1,128)} %bitcast.6, bf16[1,128]{1,0:T(2,128)(2,1)} %bitcast.7, bf16[128,256]{1,0:T(8,128)(2,1)} %down_hbm.1, ...), custom_call_target="tpu_custom_call" | custom-call | tf_op jit(solution)/shard_map/pallas_call | solution.py:448
  23.5 1.3 %copy.15 = f32[16,256]{1,0:T(8,128)} copy(f32[16,256]{1,0:T(8,128)} %shard_map.109) | data formatting | bytes 32768

commit v3 on v2

--- a/solution.py
+++ b/solution.py
@@ -107,13 +107,15 @@
     load_small[0].start()
     load_small[1].start()
     load_cond.start()
-    wf[:, 3:4, :, 0 : 3 * c1] = jnp.zeros((2, 1, c1, 3 * c1), BF16)
-    wf[:, 0:1, :, 3 * c1 :] = jnp.zeros((2, 1, c1, 3 * c1), BF16)
+    for tap in range(3):
+        upper, lower = 2 * tap * c1, (2 * tap + 1) * c1
+        wf[:, 3:4, :, upper : upper + c1] = jnp.zeros((2, 1, c1, c1), BF16)
+        wf[:, 0:1, :, lower : lower + c1] = jnp.zeros((2, 1, c1, c1), BF16)
     load_fine = [
         [
             pltpu.make_async_copy(
                 fine_hbm.at[layer, :, tap],
-                wf.at[layer, low : low + 3, :, (3 * low + tap) * c1 : (3 * low + tap + 1) * c1],
+                wf.at[layer, low : low + 3, :, (2 * tap + low) * c1 : (2 * tap + low + 1) * c1],
                 load_sem.at[6 + 6 * layer + 3 * low + tap],
             )
             for low in range(2)
@@ -219,16 +221,16 @@
     def receive_rows(level):
         links[level][2]((0, 1))
 
-    def tap_sum(parts):
-        length, depth = parts.shape[0], parts.shape[1] // 3
+    def tap_sum(before, centre, after):
+        length, depth = centre.shape
         at = lax.broadcasted_iota(jnp.int32, (8, depth), 0)
-        before = pltpu.roll(parts[:, 0:depth], 1, axis=0)
-        after = pltpu.roll(parts[:, 2 * depth :], length - 1, axis=0)
+        before = pltpu.roll(before, 1, axis=0)
+        after = pltpu.roll(after, length - 1, axis=0)
         before = jnp.concatenate([jnp.where(at == 0, 0.0, before[0:8]), before[8:]], axis=0)
         after = jnp.concatenate(
             [after[: length - 8], jnp.where(at == 7, 0.0, after[length - 8 :])], axis=0
         )
-        return before + parts[:, depth : 2 * depth] + after
+        return before + centre + after
 
     def side_terms(level, term, left, right):
         count, _, _, side_in, _ = bufs[level]
@@ -267,11 +269,14 @@
         lhs = jnp.concatenate(
             [jnp.concatenate([hp[2 * i + j] for j in range(4)], axis=1) for i in group], axis=0
         )
-        parts = dot(lhs, wf[layer].reshape(4 * c1, 6 * c1))
+        parts = [
+            dot(lhs, wf[layer, :, :, 2 * tap * c1 : 2 * (tap + 1) * c1].reshape(4 * c1, 2 * c1))
+            for tap in range(3)
+        ]
         for k, i in enumerate(group):
             for j in range(2):
                 acc0[2 * i + j] = tap_sum(
-                    parts[k * cols : (k + 1) * cols, 3 * j * c1 : 3 * (j + 1) * c1]
+                    *(p[k * cols : (k + 1) * cols, j * c1 : (j + 1) * c1] for p in parts)
                 )
 
     border = (0, pairs - 1)
@@ -281,15 +286,14 @@
     def fine_inner(layer, hp):
         for copy in load_fine[layer]:
             copy.wait()
-        for at in range(0, len(inner), 2):
-            fine_pairs(layer, hp, inner[at : at + 2])
+        fine_pairs(layer, hp, inner)
 
     def fine_sides(layer, level):
         receive_sides(level)
         side_terms(
             level, term0,
             wf[layer, 0:3, :, 0:c1].reshape(3 * c1, c1),
-            wf[layer, 0:3, :, 2 * c1 : 3 * c1].reshape(3 * c1, c1),
+            wf[layer, 0:3, :, 4 * c1 : 5 * c1].reshape(3 * c1, c1),
         )
 
     pool_at = lax.broadcasted_iota(jnp.int32, (half, 2 * cols), 1)
@@ -332,7 +336,9 @@
         )
         parts = dot(lhs, wc[...].reshape(3 * c2, 3 * c2))
         for k, i in enumerate(group):
-            acc1[i] = tap_sum(parts[k * half : (k + 1) * half])
+            acc1[i] = tap_sum(
+                *(parts[k * half : (k + 1) * half, t * c2 : (t + 1) * c2] for t in range(3))
+            )
 
     def second_start(group):
         wide = []

time: 25.1 us -> 25.3 us (level)
  Pallas kernels: 22.1 us -> 22.4 us
where the time goes in v3:
time: 25.3 us; the launch traced here: 25 us
  Pallas kernels  22.4 us (89%)
  local copies, waits for them, and re-layouts  1.32 us (5%)
  between operations  1.3 us (5%)
    pallas_call x1, Pallas kernels, per_device(): pl.pallas_call(functools.partial(kernel, sizes), out_shape=jax.ShapeDtype...  22.4 us
    unnamed x1, local copies, waits for them, and re-layouts  1.32 us

profile of v3, /device:TPU:0, one launch (start us, length us, event | category | flops | bytes accessed | tf_op | source)
XLA Modules:
  0.0 25.0 jit_solution(13075150355491804339)
XLA Ops:
  1.3 22.4 %shard_map.109 = f32[16,256]{1,0:T(8,128)} custom-call(f32[1]{0:T(128)S(6)} %copy.13.now_ref, f32[1]{0:T(128)S(6)} %copy.14.next_ref, f32[16,256]{1,0:T(8,128)} %noisy_hbm.1, f32[16,256]{1,0:T(8,128)} %draw_hbm.1, f32[1,128]{1,0:T(1,128)} %bitcast.6, bf16[1,128]{1,0:T(2,128)(2,1)} %bitcast.7, bf16[128,256]{1,0:T(8,128)(2,1)} %down_hbm.1, ...), custom_call_target="tpu_custom_call" | custom-call | tf_op jit(solution)/shard_map/pallas_call | solution.py:454
  23.7 1.3 %copy.15 = f32[16,256]{1,0:T(8,128)} copy(f32[16,256]{1,0:T(8,128)} %shard_map.109) | data formatting | bytes 32768

commit v4 on v2

--- a/solution.py
+++ b/solution.py
@@ -256,11 +256,15 @@
     load_small[1].wait()
     proj = proj_ref[...]
     load_cond.wait()
-    for row in range(height):
-        value = cond[row].astype(F32) + mine[:, row : row + 1] * proj
-        put_row(0, row, value.astype(BF16))
+    def first_rows(rows):
+        for row in rows:
+            value = cond[row].astype(F32) + mine[:, row : row + 1] * proj
+            put_row(0, row, value.astype(BF16))
+
+    first_rows((0, height - 1))
     pl.semaphore_wait(barrier, greeted)
     send_rows(0)
+    first_rows(range(1, height - 1))
     send_sides(0)
 
     def fine_pairs(layer, hp, group):

time: 25.1 us -> 25.1 us (level)
  no operation moved by 1% of the time
where the time goes in v4:
time: 25.1 us; the launch traced here: 24.8 us
  Pallas kernels  22.2 us (88%)
  local copies, waits for them, and re-layouts  1.32 us (5%)
  between operations  1.3 us (5%)
    pallas_call x1, Pallas kernels, per_device(): pl.pallas_call(functools.partial(kernel, sizes), out_shape=jax.ShapeDtype...  22.2 us
    unnamed x1, local copies, waits for them, and re-layouts  1.32 us

profile of v4, /device:TPU:0, one launch (start us, length us, event | category | flops | bytes accessed | tf_op | source)
XLA Modules:
  0.0 24.8 jit_solution(11552487293678957140)
XLA Ops:
  1.3 22.2 %shard_map.109 = f32[16,256]{1,0:T(8,128)} custom-call(f32[1]{0:T(128)S(6)} %copy.13.now_ref, f32[1]{0:T(128)S(6)} %copy.14.next_ref, f32[16,256]{1,0:T(8,128)} %noisy_hbm.1, f32[16,256]{1,0:T(8,128)} %draw_hbm.1, f32[1,128]{1,0:T(1,128)} %bitcast.6, bf16[1,128]{1,0:T(2,128)(2,1)} %bitcast.7, bf16[128,256]{1,0:T(8,128)(2,1)} %down_hbm.1, ...), custom_call_target="tpu_custom_call" | custom-call | tf_op jit(solution)/shard_map/pallas_call | solution.py:452
  23.5 1.3 %copy.15 = f32[16,256]{1,0:T(8,128)} copy(f32[16,256]{1,0:T(8,128)} %shard_map.109) | data formatting | bytes 32768
